TPU v7x, 128 devices: a whole 4x4x4 slice. The times are simulated.
128 devices in a mesh: outer: 8 (over y, x_lo), inner: 16 (over z, x_hi, core).
Axes of the slice: x: 4 (x_hi: 2, x_lo: 2; x = x_hi * 2 + x_lo), y: 4, z: 4, core: 2. Of those that a mesh axis runs over, the one named last changes fastest.
Arguments:
- activations: bfloat16 [32768, 8192], P(('outer', 'inner')), may hold values from -6 to 6
- out_grads: bfloat16 [32768, 8192], P(('outer', 'inner')), may hold values from -0.75 to 0.75
- proj_in: bfloat16 [8192, 64], replicated, may hold values from -0.0625 to 0.0625
- proj_out: bfloat16 [8192, 32], replicated, may hold values from -0.0625 to 0.0625
- lengths: int32 [2048], P(('outer', 'inner')), may hold values from 1 to 16
- factor: bfloat16 [2048, 2048], P('inner'), may hold values from -0.125 to 0.125
- store: bfloat16 [393216, 2048], P(('outer', 'inner')), may hold values from -0.125 to 0.125
Outputs:
- scores: bfloat16 [1024, 393216], P(None, ('outer', 'inner'))
All inputs are finite; a program needn't handle non-finite values.
Results may differ from a plain program's by a relative error of at most 0.008.
Values may be sent and summed in bfloat16 or wider, within the bound.
A program may use at most 128 MiB of HBM per device.

v0:
```python
import jax
import jax.numpy as jnp
from jax import lax
from jax.sharding import PartitionSpec as P

RIN = 64
ROUT = 32
SEQ_LEN = 16


def shards(activations, out_grads, proj_in, proj_out, lengths, factor, store):
    tok_rows = activations.shape[0]
    seq_count = lengths.shape[0]
    pair_count = seq_count // 2
    in_proj = jnp.dot(activations, proj_in, preferred_element_type=jnp.float32).astype(jnp.bfloat16)
    out_full = jnp.dot(out_grads, proj_out, preferred_element_type=jnp.float32)
    index = lax.iota(jnp.int32, tok_rows)
    position = index % SEQ_LEN
    sequence = index // SEQ_LEN
    match = sequence[:, None] == lax.iota(jnp.int32, seq_count)[None, :]
    tok_length = jnp.sum(jnp.where(match, lengths[None, :], 0), axis=1)
    out_proj = jnp.where((position < tok_length)[:, None], out_full, 0.0).astype(jnp.bfloat16)
    left = out_proj.reshape(pair_count, 2 * SEQ_LEN, ROUT)
    right = in_proj.reshape(pair_count, 2 * SEQ_LEN, RIN)
    pair_grads = jnp.einsum("pta,ptb->pab", left, right, preferred_element_type=jnp.float32)
    pair_grads = pair_grads.reshape(pair_count, RIN * ROUT).astype(jnp.bfloat16)
    whitened = jnp.dot(
        pair_grads,
        lax.all_gather(factor, "inner", axis=0, tiled=True),
        preferred_element_type=jnp.float32,
    )
    queries = whitened.astype(jnp.bfloat16)
    return lax.dot_general(
        lax.all_gather(queries, ("outer", "inner"), axis=0, tiled=True),
        store,
        (((1,), (1,)), ((), ())),
        preferred_element_type=jnp.float32,
    ).astype(jnp.bfloat16)


def solution(mesh):
    in_specs = (
        P(("outer", "inner"), None),
        P(("outer", "inner"), None),
        P(),
        P(),
        P(("outer", "inner")),
        P("inner", None),
        P(("outer", "inner"), None),
    )
    out_specs = P(None, ("outer", "inner"))
    return jax.shard_map(shards, mesh=mesh, in_specs=in_specs, out_specs=out_specs, check_vma=False)
```

profile of v0, /device:TPU:1, one launch (start us, length us, event | category | flops | bytes accessed | tf_op | source)
XLA Modules:
  0.0 312.1 jit_solution(16937480270073581595)
XLA Ops:
  6.5 0.0 copy-start
  6.5 0.0 copy-start.2
  6.5 0.0 copy-start.1
  6.5 0.0 all-gather.3.cloned.1.call-start
  6.5 0.7 all-gather.3.cloned.1.call-update
  7.3 0.0 all-gather.5.cloned.1.call-start
  7.3 0.5 copy-done
  7.8 3.6 %convolution_convert_fusion.3 = bf16[256,64]{0,1:T(8,128)(2,1)S(1)} fusion(bf16[256,8192]{1,0:T(8,128)(2,1)} %param.7, bf16[8192,64]{0,1:T(8,128)(2,1)S(1)} %copy-done), kind=kOutput, calls=%fused_computation.3 | convolution fusion | flops 268451840 | bytes 5275648 | tf_op jit(solution)/shard_map/dot_general | solution.py:15
  11.3 0.1 copy.12
  11.5 0.0 copy-done.2
  11.5 0.1 select_reduce_fusion
  11.6 0.0 copy-done.1
  11.6 3.5 %fusion = bf16[256,32]{0,1:T(8,128)(2,1)S(1)} fusion(bf16[256,8192]{1,0:T(8,128)(2,1)} %param.8, bf16[8192,32]{0,1:T(8,128)(2,1)S(1)} %copy-done.1, pred[256]{0:T(512)(128)(4,1)S(1)} %fusion.2), kind=kOutput, calls=%fused_computation.5 | convolution fusion | flops 134234112 | bytes 4735232 | tf_op jit(solution)/shard_map/dot_general | solution.py:16
  15.1 0.1 reshape.34
  15.2 0.1 convolution_convert_fusion.2
  15.4 0.1 convert_element_type.21
  15.5 71.1 %all-gather.3.cloned.1.call-done = bf16[2048,2048]{1,0:T(8,128)(2,1)} async-done(((bf16[128,2048]{1,0:T(8,128)(2,1)}), bf16[2048,2048]{1,0:T(8,128)(2,1)}) %all-gather.3.cloned.1.call-update) | async-done | bytes 8388624 | tf_op jit(solution)/shard_map/all_gather | solution.py:29
  86.6 5.2 %convolution_convert_fusion.1 = bf16[8,2048]{1,0:T(8,128)(2,1)} fusion(bf16[8,2048]{1,0:T(8,128)(2,1)S(1)} %convert_element_type.21, bf16[2048,2048]{1,0:T(8,128)(2,1)} %all-gather.3.cloned.1.call-done), kind=kOutput, calls=%fused_computation.1 | convolution fusion | flops 67125248 | bytes 8454144 | tf_op jit(solution)/shard_map/dot_general | solution.py:27
  91.8 0.0 all-gather.5.cloned.1.call-update
  91.9 195.1 %all-gather.5.cloned.1.call-done = bf16[1024,2048]{1,0:T(8,128)(2,1)} async-done(((bf16[8,2048]{1,0:T(8,128)(2,1)}), bf16[1024,2048]{1,0:T(8,128)(2,1)}) %all-gather.5.cloned.1.call-update) | async-done | bytes 4194320 | tf_op jit(solution)/shard_map/all_gather | solution.py:34
  286.9 18.4 %convolution_convert_fusion = bf16[1024,3072]{1,0:T(8,128)(2,1)} fusion(bf16[1024,2048]{1,0:T(8,128)(2,1)} %all-gather.5.cloned.1.call-done, bf16[3072,2048]{1,0:T(8,128)(2,1)} %param.13), kind=kOutput, calls=%fused_computation | convolution fusion | flops 12888047616 | bytes 23068672 | tf_op jit(solution)/shard_map/dot_general | solution.py:33
  (2 shorter events, 0.0 us)
Async XLA Ops:
  6.5 1.2 copy-start
  6.5 4.9 %copy-start.2 = (s32[16]{0:T(128)S(1)}, s32[16]{0:T(128)}, u32[]{:S(2)}) copy-start(s32[16]{0:T(128)} %param.11) | copy-start | bytes 196
  6.5 5.0 %copy-start.1 = (bf16[8192,32]{0,1:T(8,128)(2,1)S(1)}, bf16[8192,32]{0,1:T(8,128)(2,1)}, u32[]{:S(2)}) copy-start(bf16[8192,32]{0,1:T(8,128)(2,1)} %param.10) | copy-start | bytes 1572868
  6.5 80.1 %all-gather.3.cloned.1.call-start = ((), (), s32[]{:S(2)}) async-start(), calls=%async_computation | async-start | bytes 8912896 | tf_op jit(solution)/shard_map/all_gather | solution.py:29
  7.3 279.6 %all-gather.5.cloned.1.call-start = ((), (), s32[]{:S(2)}) async-start(), calls=%async_computation.1 | async-start | bytes 4227072 | tf_op jit(solution)/shard_map/all_gather | solution.py:34
Sparse Core Ops, SparseCore 0:
  9.8 76.7 all-gather.2
  92.0 194.8 all-gather.4
where the time goes:
time: 312 us
  waiting for transfers between devices  267 us (86%)
  matrix products  30.9 us (10%)
  between operations  13.4 us (4%)
    all_gather x1, waiting for transfers between devices, shards(): lax.all_gather(queries, ('outer', 'inner'), axis=0, tiled=True)  195 us
    all_gather x1, waiting for transfers between devices, shards(): lax.all_gather(factor, 'inner', axis=0, tiled=True)  71.1 us
    dot_general x1, matrix products, shards(): lax.dot_general(lax.all_gather(queries, ('outer', 'inner'), axis=0, tiled...  18.4 us
  transfers between devices with their start and end apart: 2, of which 2 were waited for; matrix products, arithmetic and copies ran while one was open for 2% of the time, Pallas kernels for 0%

commit v1 on v0

v1 whole, which is shorter than its diff:
```python
import functools

import jax
import jax.numpy as jnp
from jax import lax
from jax.experimental import pallas as pl
from jax.experimental.pallas import tpu as pltpu
from jax.sharding import PartitionSpec as P

D = 8192
RIN = 64
ROUT = 32
K = 2048
SEQ = 16
TOK = 256
NSEQ = 16
NP = 8
COLS = 128
CHUNK = 1024
NCHUNK = D // CHUNK
BF = jnp.bfloat16
F32 = jnp.float32
MESH = pl.DeviceIdType.MESH

PARTS = ((0, 48, "zxy"), (48, 48, "xyz"), (96, 32, "yzx"))


def device(pos, core):
    outer = pos["y"] * 2 + lax.rem(pos["x"], 2)
    inner = (pos["z"] * 2 + lax.div(pos["x"], 2)) * 2 + core
    return outer, inner


def gather_kernel(act, grad, w_in, w_out, lengths_hbm, factor, store, q0, q1, q2, store_v,
                  act_v, grad_v, w_in_v, w_out_v, fcol, pg, lengths,
                  load_sem, store_sem, length_sem, own_f_sem, f_send, f_recv, p_send, p_recv, s_send, s_recv,
                  g1_send, g1_recv, g2_send, g2_recv, g3_send, g3_recv, c_send, c_recv):
    qs = (q0, q1, q2)
    outer = lax.axis_index("outer")
    inner = lax.axis_index("inner")
    core = lax.rem(inner, 2)
    spot = lax.div(inner, 2)
    pos = {"y": lax.div(outer, 2), "z": lax.div(inner, 4), "x": lax.rem(spot, 2) * 2 + lax.rem(outer, 2)}
    sibling = (outer, spot * 2 + 1 - core)

    def near(axis, step):
        moved = dict(pos)
        moved[axis] = lax.rem(pos[axis] + step, 4)
        return device(moved, core)

    length_copy = pltpu.make_async_copy(lengths_hbm, lengths, length_sem)
    length_copy.start()
    loads = []
    for k in range(NCHUNK):
        cols = pl.ds(k * CHUNK, CHUNK)
        row = []
        for n, (src, dst) in enumerate(((w_in, w_in_v), (act, act_v), (w_out, w_out_v), (grad, grad_v))):
            copy = pltpu.make_async_copy(src.at[:, cols], dst.at[:, cols], load_sem.at[k, n])
            copy.start()
            row.append(copy)
        loads.append(row)

    store_copy = pltpu.make_async_copy(store, store_v, store_sem)
    store_copy.start()

    barrier = pltpu.get_barrier_semaphore()
    peers = [(outer, lax.rem(inner + k, 16)) for k in range(1, 16)]
    peers += [near("y", 1), near("y", 2), near("y", 3), near("x", 1), near("x", 3)]
    for peer in peers:
        pl.semaphore_signal(barrier, inc=1, device_id=peer, device_id_type=MESH)
    pl.semaphore_wait(barrier, len(peers))

    def remote(src, dst, send, recv, target):
        return pltpu.make_async_remote_copy(src_ref=src, dst_ref=dst, send_sem=send, recv_sem=recv,
                                            device_id=target, device_id_type=MESH)

    def columns(who):
        return factor.at[:, pl.ds(pl.multiple_of(who * COLS, COLS), COLS)]

    f_copies = []
    for k in range(1, 16):
        to = lax.rem(inner + k, 16)
        copy = remote(columns(to), fcol.at[inner], f_send.at[k], f_recv.at[k], (outer, to))
        copy.start()
        f_copies.append(copy)
    own_f = pltpu.make_async_copy(columns(inner), fcol.at[inner], own_f_sem)
    own_f.start()

    ins = jnp.zeros((TOK, 2 * RIN), F32)
    outs = jnp.zeros((TOK, ROUT), F32)
    across = (((1,), (1,)), ((), ()))
    for k in range(NCHUNK):
        cols = pl.ds(k * CHUNK, CHUNK)
        for copy in loads[k]:
            copy.wait()
        w = w_in_v[:, cols]
        ins += lax.dot_general(act_v[:, cols], jnp.concatenate([w, w], axis=0), across, preferred_element_type=F32)
        outs += lax.dot_general(grad_v[:, cols], w_out_v[:, cols], across, preferred_element_type=F32)

    length_copy.wait()
    position = lax.broadcasted_iota(jnp.int32, (SEQ, ROUT), 0)
    kept = [jnp.where(position < lengths[s], outs[s * SEQ:(s + 1) * SEQ], 0.0) for s in range(NSEQ)]
    outs = jnp.concatenate(kept, axis=0).astype(BF)
    ins = ins.astype(BF).astype(F32)
    for j in range(K // 128):
        a = lax.broadcasted_iota(jnp.int32, (ROUT, 128), 0)
        b = lax.broadcasted_iota(jnp.int32, (ROUT, 128), 1)
        pick = jnp.where(a == 2 * j + lax.div(b, RIN), 1.0, 0.0).astype(BF)
        wide = jnp.dot(outs, pick, preferred_element_type=F32)
        sums = jnp.sum((wide * ins).reshape(NP, 2 * SEQ, 128), axis=1)
        pg[inner, :, j * 128:(j + 1) * 128] = sums.astype(BF)

    p_copies = []
    for k in range(1, 8):
        to = lax.rem(spot + k, 8) * 2 + core
        copy = remote(pg.at[inner], pg.at[inner], p_send.at[k], p_recv.at[k], (outer, to))
        copy.start()
        p_copies.append(copy)
    s_copies = [remote(pg.at[inner], pg.at[inner], s_send.at[0], s_recv.at[0], sibling)]
    s_copies[0].start()
    for k in range(1, 8):
        p_copies[k - 1].wait_recv()
        slot = lax.rem(spot + 8 - k, 8) * 2 + core
        copy = remote(pg.at[slot], pg.at[slot], s_send.at[k], s_recv.at[k], sibling)
        copy.start()
        s_copies.append(copy)
    own_f.wait()
    for copy in f_copies:
        copy.wait_recv()
    for copy in s_copies:
        copy.wait_recv()

    white = jnp.dot(pg[...].reshape(16 * NP, K), fcol[...].reshape(K, COLS), preferred_element_type=F32).astype(BF)
    for q, (start, rows, order) in zip(qs, PARTS):
        q[core, pos[order[2]], pos[order[1]], pos[order[0]]] = white[start:start + rows]

    sends = list(p_copies) + list(f_copies) + list(s_copies)

    def go(*args):
        copy = remote(*args)
        copy.start()
        sends.append(copy)
        return copy

    def along(order, n, step):
        return lax.rem(pos[order[n]] + step, 4)

    first = []
    for p, (q, (_, _, order)) in enumerate(zip(qs, PARTS)):
        mine = q.at[core, pos[order[2]], pos[order[1]], pos[order[0]]]
        first.append([go(mine, mine, g1_send.at[p, d - 1], g1_recv.at[p, d - 1], near(order[0], d)) for d in (1, 3, 2)])

    def spread(p, axis, view, send, recv):
        halves = (pl.ds(0, 2), pl.ds(2, 2))
        copies = {}
        for name, step, half, n in (("r0", 1, 0, 0), ("l1", 3, 1, 1), ("r1", 1, 1, 2), ("l0", 3, 0, 3)):
            mine = view(0).at[halves[half]]
            copies[name] = go(mine, mine, send.at[p, n], recv.at[p, n], near(axis, step))
        return copies

    def relay(p, axis, view, send, recv, copies):
        for name, came, half, step, n in (("r0", 3, 0, 1, 4), ("l1", 1, 1, 3, 5)):
            copies[name].wait_recv()
            part = view(came).at[pl.ds(2 * half, 2)]
            copies["f" + name] = go(part, part, send.at[p, n], recv.at[p, n], near(axis, step))

    def view2(p):
        q, order = qs[p], PARTS[p][2]
        return lambda step: q.at[core, pos[order[2]], along(order, 1, step)]

    def view3(p):
        q, order = qs[p], PARTS[p][2]
        return lambda step: q.at[core, along(order, 2, step)]

    second, third, cross = [], [], []
    for p in range(3):
        for copy in first[p]:
            copy.wait_recv()
        second.append(spread(p, PARTS[p][2][1], view2(p), g2_send, g2_recv))
    for p in range(3):
        relay(p, PARTS[p][2][1], view2(p), g2_send, g2_recv, second[p])

    def over(p, step):
        part = view3(p)(step)
        cross.append(go(part, part, c_send.at[p, step], c_recv.at[p, step], sibling))

    for p in range(3):
        for name in ("r1", "l0", "fr0", "fl1"):
            second[p][name].wait_recv()
        third.append(spread(p, PARTS[p][2][2], view3(p), g3_send, g3_recv))
        over(p, 0)
    for p in range(3):
        relay(p, PARTS[p][2][2], view3(p), g3_send, g3_recv, third[p])
    for p in range(3):
        third[p]["r1"].wait_recv()
        over(p, 3)
        third[p]["l0"].wait_recv()
        over(p, 1)
    for p in range(3):
        third[p]["fr0"].wait_recv()
        third[p]["fl1"].wait_recv()
        over(p, 2)
    for copy in cross:
        copy.wait_recv()
    store_copy.wait()
    for copy in sends:
        copy.wait_send()


def score_kernel(q0, q1, q2, store, out):
    qs = (q0, q1, q2)
    rows = []
    for y in range(4):
        for xlo in range(2):
            for q, (_, _, order) in zip(qs, PARTS):
                cols = []
                for z in range(4):
                    for xhi in range(2):
                        for core in range(2):
                            at = {"x": xhi * 2 + xlo, "y": y, "z": z}
                            cols.append(q[core, at[order[2]], at[order[1]], at[order[0]]])
                rows.append(jnp.concatenate(cols, axis=1))
    lhs = jnp.concatenate(rows, axis=0)
    some = store[pl.ds(pl.multiple_of(pl.program_id(0) * 256, 256), 256), :]
    out[...] = lax.dot_general(lhs, some, (((1,), (1,)), ((), ())), preferred_element_type=F32).astype(BF)


def shards(activations, out_grads, proj_in, proj_out, lengths, factor, store):
    dma = pltpu.SemaphoreType.DMA
    hbm = pl.BlockSpec(memory_space=pltpu.HBM)
    vmem = pl.BlockSpec(memory_space=pltpu.VMEM)
    qs = pl.pallas_call(
        gather_kernel,
        out_shape=[pltpu.VMEM((2, 4, 4, 4, rows, COLS), BF) for _, rows, _ in PARTS] + [pltpu.VMEM(store.shape, BF)],
        in_specs=[hbm] * 7,
        out_specs=[vmem] * 4,
        scratch_shapes=[
            pltpu.VMEM((TOK, D), BF), pltpu.VMEM((TOK, D), BF),
            pltpu.VMEM((RIN, D), BF), pltpu.VMEM((ROUT, D), BF),
            pltpu.VMEM((16, 128, COLS), BF), pltpu.VMEM((16, NP, K), BF), pltpu.SMEM((NSEQ,), jnp.int32),
            dma((NCHUNK, 4)), dma, dma, dma, dma((16,)), dma((16,)), dma((8,)), dma((8,)), dma((8,)), dma((8,)),
            dma((3, 3)), dma((3, 3)), dma((3, 6)), dma((3, 6)), dma((3, 6)), dma((3, 6)), dma((3, 4)), dma((3, 4)),
        ],
        compiler_params=pltpu.CompilerParams(collective_id=0, has_side_effects=True, vmem_limit_bytes=32 << 20),
        name="gather",
    )(*[pltpu.with_memory_space_constraint(v, pltpu.HBM)
        for v in (activations, out_grads, proj_in.T, proj_out.T, lengths, factor, store)])
    n = store.shape[0]
    return pl.pallas_call(
        score_kernel,
        out_shape=jax.ShapeDtypeStruct((1024, n), BF),
        grid=(n // 256,),
        in_specs=[vmem] * 4,
        out_specs=pl.BlockSpec((1024, 256), lambda i: (0, i)),
        compiler_params=pltpu.CompilerParams(vmem_limit_bytes=32 << 20),
        name="score",
    )(*qs)


def solution(mesh):
    in_specs = (
        P(("outer", "inner"), None),
        P(("outer", "inner"), None),
        P(),
        P(),
        P(("outer", "inner")),
        P("inner", None),
        P(("outer", "inner"), None),
    )
    out_specs = P(None, ("outer", "inner"))
    return jax.shard_map(shards, mesh=mesh, in_specs=in_specs, out_specs=out_specs, check_vma=False)
```

time: 312 us -> 61 us (0.20)
  waiting for transfers between devices: 267 us -> 0 us
  Pallas kernels: 0 us -> 60.9 us
  matrix products: 30.9 us -> 0 us
  between operations: 13.4 us -> 0.01 us
    all_gather x2 -> x0, waiting for transfers between devices: 266 us -> none  [the longest x1 195 us: shards(): lax.all_gather(queries, ('outer', 'inner'), axis=0, tiled=True)]
    pallas_call x0 -> x2, Pallas kernels: none -> 60.9 us  [the longest x1 44.5 us: shards(): pl.pallas_call(gather_kernel, out_shape=[pltpu.VMEM((2, 4, 4, 4, rows, CO...]
    dot_general x5 -> x0, matrix products: 30.9 us -> none  [the longest x1 18.4 us: shards(): lax.dot_general(lax.all_gather(queries, ('outer', 'inner'), axis=0, tiled...]
  transfers between devices with their start and end apart: 2 -> 0, of which waited for: 2 -> 0; matrix products, arithmetic and copies ran while one was open for 2% -> 0% of each run, Pallas kernels for 0% -> 0%
where the time goes in v1:
time: 61 us; the launch traced here: 60.9 us
  Pallas kernels  60.9 us (100%)
    pallas_call x1, Pallas kernels, shards(): pl.pallas_call(gather_kernel, out_shape=[pltpu.VMEM((2, 4, 4, 4, rows, CO...  44.5 us
    pallas_call x1, Pallas kernels, shards(): pl.pallas_call(score_kernel, out_shape=jax.ShapeDtypeStruct((1024, n), BF...  16.3 us

profile of v1, /device:TPU:1, one launch (start us, length us, event | category | flops | bytes accessed | tf_op | source)
XLA Modules:
  0.0 60.9 jit_solution(14863799682455057489)
XLA Ops:
  0.0 44.5 %gather.1 = (bf16[2,4,4,4,48,128]{5,4,3,2,1,0:T(8,128)(2,1)S(1)}, bf16[2,4,4,4,48,128]{5,4,3,2,1,0:T(8,128)(2,1)S(1)}, bf16[2,4,4,4,32,128]{5,4,3,2,1,0:T(8,128)(2,1)S(1)}, bf16[3072,2048]{1,0:T(8,128)(2,1)S(1)}) custom-call(bf16[256,8192]{1,0:T(8,128)(2,1)} %act.1, bf16[256,8192]{1,0:T(8,128)(2,1)} %grad.1, bf16[64,8192]{1,0:T(8,128)(2,1)} %bitcast.2, ...), custom_call_target="tpu_custom_call" | custom-call | tf_op jit(solution)/shard_map/gather/pallas_call | solution.py:232
  44.5 16.3 %score.1 = bf16[1024,3072]{1,0:T(8,128)(2,1)} custom-call(bf16[2,4,4,4,48,128]{5,4,3,2,1,0:T(8,128)(2,1)S(1)} %get-tuple-element.9.q0, bf16[2,4,4,4,48,128]{5,4,3,2,1,0:T(8,128)(2,1)S(1)} %get-tuple-element.10.q1, bf16[2,4,4,4,32,128]{5,4,3,2,1,0:T(8,128)(2,1)S(1)} %get-tuple-element.11.q2, bf16[3072,2048]{1,0:T(8,128)(2,1)S(1)} %get-tuple-element.12.store), custom_call_target="tpu_custom_call" | custom-call | tf_op jit(solution)/shard_map/score/pallas_call | solution.py:249

commit v2 on v0

v2 whole, which is shorter than its diff:
```python
import jax
import jax.numpy as jnp
from jax import lax
from jax.experimental import pallas as pl
from jax.experimental.pallas import tpu as pltpu
from jax.sharding import PartitionSpec as P

D = 8192
RIN = 64
ROUT = 32
K = 2048
SEQ = 16
TOK = 256
NSEQ = 16
NP = 8
COLS = 128
HALF = 64
CHUNK = 1024
NCHUNK = D // CHUNK
STORE = 3072
WIDE = 1024
BLOCK = 512
BF = jnp.bfloat16
F32 = jnp.float32
MESH = pl.DeviceIdType.MESH
ACROSS = (((1,), (1,)), ((), ()))


def mod(a, b):
    return lax.rem(a, b)


def offset(j):
    half = j // 2
    return (half if half < 2 else 5 - half) if isinstance(j, int) else jnp.where(half < 2, half, 5 - half), j % 2


def gather_kernel(act, grad, w_in, w_out, lengths_hbm, factor, store, qa, total, store_v,
                  qb, act_v, grad_v, w_in_v, w_out_v, fcol, pg, lengths,
                  load_sem, store_sem, length_sem, own_f_sem, f_send, f_recv, p_send, p_recv, s_send, s_recv,
                  an_send, an_recv, bf_send, bf_recv, af_send, af_recv, bn_send, bn_recv,
                  ac_send, ac_recv, bc_send, bc_recv):
    outer = lax.axis_index("outer")
    inner = lax.axis_index("inner")
    core = mod(inner, 2)
    spot = lax.div(inner, 2)
    y, xlo = lax.div(outer, 2), mod(outer, 2)
    z, xhi = lax.div(spot, 2), mod(spot, 2)
    gx = mod(xlo + xhi, 2)
    sibling = (outer, spot * 2 + 1 - core)
    group_a = y * 2 + gx
    group_b = y * 2 + 1 - gx

    def near(j, flip=0):
        dz, dx = offset(j)
        hi = mod(xhi + dx, 2)
        return y * 2 + mod(gx + hi, 2), (mod(z + dz, 4) * 2 + hi) * 2 + mod(core + flip, 2)

    def near_spot(j):
        dz, dx = offset(j)
        return mod(z + 4 - dz, 4) * 2 + mod(xhi + dx, 2)

    def far(j):
        dy, dx = offset(j)
        return mod(y + dy, 4) * 2 + mod(gx + dx + xhi, 2), inner

    def far_group(j):
        dy, dx = offset(j)
        return mod(y + 4 - dy, 4) * 2 + mod(gx + dx, 2)

    length_copy = pltpu.make_async_copy(lengths_hbm, lengths, length_sem)
    length_copy.start()
    loads = []
    for k in range(NCHUNK):
        cols = pl.ds(k * CHUNK, CHUNK)
        row = []
        for n, (src, dst) in enumerate(((w_in, w_in_v), (act, act_v), (w_out, w_out_v), (grad, grad_v))):
            copy = pltpu.make_async_copy(src.at[:, cols], dst.at[:, cols], load_sem.at[k, n])
            copy.start()
            row.append(copy)
        loads.append(row)

    barrier = pltpu.get_barrier_semaphore()
    peers = [near(j, flip) for j in range(8) for flip in range(2) if j + flip] + [far(j) for j in range(1, 8)]
    for peer in peers:
        pl.semaphore_signal(barrier, inc=1, device_id=peer, device_id_type=MESH)
    total[...] = jnp.zeros(total.shape, F32)
    pl.semaphore_wait(barrier, len(peers))

    def remote(src, send, recv, target, dst=None):
        return pltpu.make_async_remote_copy(src_ref=src, dst_ref=src if dst is None else dst, send_sem=send, recv_sem=recv,
                                            device_id=target, device_id_type=MESH)

    sends = []

    def go(*args):
        copy = remote(*args)
        copy.start()
        sends.append(copy)
        return copy

    def columns(who):
        return factor.at[:, pl.ds(pl.multiple_of(who * COLS, COLS), COLS)]

    f_copies = []
    for n in range(1, 16):
        to = near(n // 2, n % 2)
        f_copies.append(go(columns(to[1]), f_send.at[n], f_recv.at[n], to, fcol.at[inner]))
    own_f = pltpu.make_async_copy(columns(inner), fcol.at[inner], own_f_sem)
    own_f.start()

    ins = jnp.zeros((TOK, 2 * RIN), F32)
    outs = jnp.zeros((TOK, ROUT), F32)
    for k in range(NCHUNK):
        cols = pl.ds(k * CHUNK, CHUNK)
        for copy in loads[k]:
            copy.wait()
        if k == NCHUNK - 1:
            store_copy = pltpu.make_async_copy(store, store_v, store_sem)
            store_copy.start()
        w = w_in_v[:, cols]
        ins += lax.dot_general(act_v[:, cols], jnp.concatenate([w, w], axis=0), ACROSS, preferred_element_type=F32)
        outs += lax.dot_general(grad_v[:, cols], w_out_v[:, cols], ACROSS, preferred_element_type=F32)

    length_copy.wait()
    position = lax.broadcasted_iota(jnp.int32, (SEQ, ROUT), 0)
    kept = [jnp.where(position < lengths[s], outs[s * SEQ:(s + 1) * SEQ], 0.0) for s in range(NSEQ)]
    outs = jnp.concatenate(kept, axis=0).astype(BF)
    ins = ins.astype(BF).astype(F32)
    own_slot = xhi * 8 + z * 2 + core
    for j in range(K // 128):
        a = lax.broadcasted_iota(jnp.int32, (ROUT, 128), 0)
        b = lax.broadcasted_iota(jnp.int32, (ROUT, 128), 1)
        pick = jnp.where(a == 2 * j + lax.div(b, RIN), 1.0, 0.0).astype(BF)
        wide = jnp.dot(outs, pick, preferred_element_type=F32)
        sums = jnp.sum((wide * ins).reshape(NP, 2 * SEQ, 128), axis=1)
        pg[own_slot, :, j * 128:(j + 1) * 128] = sums.astype(BF)

    p_copies = [go(pg.at[own_slot], p_send.at[j], p_recv.at[j], near(j)) for j in range(1, 8)]
    s_copies = [go(pg.at[own_slot], s_send.at[0], s_recv.at[0], sibling)]
    for j in range(1, 8):
        p_copies[j - 1].wait_recv()
        from_spot = near_spot(j)
        slot = mod(from_spot, 2) * 8 + lax.div(from_spot, 2) * 2 + core
        s_copies.append(go(pg.at[slot], s_send.at[j], s_recv.at[j], sibling))
    own_f.wait()
    for copy in f_copies:
        copy.wait_recv()
    for copy in s_copies:
        copy.wait_recv()

    white = jnp.dot(pg[...].reshape(16 * NP, K), fcol[...].reshape(K, COLS), preferred_element_type=F32).astype(BF)
    qa[core, group_a, spot] = white[:HALF]
    qb[core, spot, group_b] = white[HALF:]

    a_near, b_far = [], []
    for j in range(1, 8):
        a_near.append(go(qa.at[core, group_a, spot], an_send.at[j], an_recv.at[j], near(j)))
        b_far.append(go(qb.at[core, spot, group_b], bf_send.at[j], bf_recv.at[j], far(j)))

    def a_over(j):
        return remote(qa.at[core, far_group(j)], ac_send.at[j], ac_recv.at[j], sibling)

    def b_over(j):
        return remote(qb.at[core, near_spot(j)], bc_send.at[j], bc_recv.at[j], sibling)

    def a_far(j):
        return remote(qa.at[core, group_a], af_send.at[j], af_recv.at[j], far(j))

    def b_near(j):
        return remote(qb.at[core, spot], bn_send.at[j], bn_recv.at[j], near(j))

    for copy in b_far:
        copy.wait_recv()
    for j in range(1, 8):
        b_near(j).start()
    b_over(0).start()
    for copy in a_near:
        copy.wait_recv()
    for j in range(1, 8):
        a_far(j).start()
    a_over(0).start()
    store_copy.wait()

    def step(j, carry):
        @pl.when(j < 7)
        def _():
            b_near(j + 1).wait_recv()
            b_over(j + 1).start()
            a_far(j + 1).wait_recv()
            a_over(j + 1).start()

        b_over(j).wait_recv()
        k8 = near_spot(j)
        lhs = jnp.concatenate([qb[0, k8].reshape(8 * HALF, COLS), qb[1, k8].reshape(8 * HALF, COLS)], axis=1)
        cols = pl.ds(pl.multiple_of(k8 * 2 * COLS, 2 * COLS), 2 * COLS)
        for n in range(STORE // WIDE):
            some = slice(n * WIDE, (n + 1) * WIDE)
            total[:, some] += lax.dot_general(lhs, store_v[some, cols], ACROSS, preferred_element_type=F32)
        return carry

    lax.fori_loop(0, 8, step, 0)

    def finish(j, carry):
        a_over(j).wait()
        b_over(j).wait_send()

        @pl.when(j > 0)
        def _():
            a_far(j).wait_send()
            b_near(j).wait_send()
        return carry

    lax.fori_loop(0, 8, finish, 0)
    for copy in sends:
        copy.wait_send()


def score_kernel(qa, total, store, out):
    some = pl.ds(pl.multiple_of(pl.program_id(0) * BLOCK, BLOCK), BLOCK)
    rows = [jnp.concatenate([qa[c, g, k] for k in range(8) for c in range(2)], axis=1) for g in range(8)]
    lhs = jnp.concatenate(rows, axis=0)
    first = lax.dot_general(lhs, store[some, :], ACROSS, preferred_element_type=F32).astype(BF)
    second = total[:, some].astype(BF)
    for n in range(32):
        part = slice(16 * n, 16 * n + 16)
        out[32 * n:32 * n + 16, :] = first[part]
        out[32 * n + 16:32 * n + 32, :] = second[part]


def shards(activations, out_grads, proj_in, proj_out, lengths, factor, store):
    dma = pltpu.SemaphoreType.DMA
    hbm = pl.BlockSpec(memory_space=pltpu.HBM)
    vmem = pl.BlockSpec(memory_space=pltpu.VMEM)
    parts = pl.pallas_call(
        gather_kernel,
        out_shape=[pltpu.VMEM((2, 8, 8, HALF, COLS), BF), pltpu.VMEM((8 * HALF, STORE), F32), pltpu.VMEM((STORE, K), BF)],
        in_specs=[hbm] * 7,
        out_specs=[vmem] * 3,
        scratch_shapes=[
            pltpu.VMEM((2, 8, 8, HALF, COLS), BF),
            pltpu.VMEM((TOK, D), BF), pltpu.VMEM((TOK, D), BF),
            pltpu.VMEM((RIN, D), BF), pltpu.VMEM((ROUT, D), BF),
            pltpu.VMEM((16, 128, COLS), BF), pltpu.VMEM((16, NP, K), BF), pltpu.SMEM((NSEQ,), jnp.int32),
            dma((NCHUNK, 4)), dma, dma, dma, dma((16,)), dma((16,)),
        ] + [dma((8,))] * 16,
        compiler_params=pltpu.CompilerParams(collective_id=0, has_side_effects=True, vmem_limit_bytes=32 << 20),
        name="gather",
    )(*[pltpu.with_memory_space_constraint(v, pltpu.HBM)
        for v in (activations, out_grads, proj_in.T, proj_out.T, lengths, factor, store)])
    return pl.pallas_call(
        score_kernel,
        out_shape=jax.ShapeDtypeStruct((16 * HALF, STORE), BF),
        grid=(STORE // BLOCK,),
        in_specs=[vmem] * 3,
        out_specs=pl.BlockSpec((16 * HALF, BLOCK), lambda i: (0, i)),
        compiler_params=pltpu.CompilerParams(vmem_limit_bytes=32 << 20),
        name="score",
    )(*parts)


def solution(mesh):
    in_specs = (
        P(("outer", "inner"), None),
        P(("outer", "inner"), None),
        P(),
        P(),
        P(("outer", "inner")),
        P("inner", None),
        P(("outer", "inner"), None),
    )
    out_specs = P(None, ("outer", "inner"))
    return jax.shard_map(shards, mesh=mesh, in_specs=in_specs, out_specs=out_specs, check_vma=False)
```

time: 312 us -> 55.2 us (0.18)
  waiting for transfers between devices: 267 us -> 0 us
  Pallas kernels: 0 us -> 55.1 us
  matrix products: 30.9 us -> 0 us
  between operations: 13.4 us -> 0.01 us
    all_gather x2 -> x0, waiting for transfers between devices: 266 us -> none  [the longest x1 195 us: shards(): lax.all_gather(queries, ('outer', 'inner'), axis=0, tiled=True)]
    pallas_call x0 -> x2, Pallas kernels: none -> 55.1 us  [the longest x1 46.4 us: shards(): pl.pallas_call(gather_kernel, out_shape=[pltpu.VMEM((2, 8, 8, HALF, COLS)...]
    dot_general x5 -> x0, matrix products: 30.9 us -> none  [the longest x1 18.4 us: shards(): lax.dot_general(lax.all_gather(queries, ('outer', 'inner'), axis=0, tiled...]
  transfers between devices with their start and end apart: 2 -> 0, of which waited for: 2 -> 0; matrix products, arithmetic and copies ran while one was open for 2% -> 0% of each run, Pallas kernels for 0% -> 0%
where the time goes in v2:
time: 55.2 us; the launch traced here: 55.1 us
  Pallas kernels  55.1 us (100%)
    pallas_call x1, Pallas kernels, shards(): pl.pallas_call(gather_kernel, out_shape=[pltpu.VMEM((2, 8, 8, HALF, COLS)...  46.4 us
    pallas_call x1, Pallas kernels, shards(): pl.pallas_call(score_kernel, out_shape=jax.ShapeDtypeStruct((16 * HALF, S...  8.74 us

profile of v2, /device:TPU:1, one launch (start us, length us, event | category | flops | bytes accessed | tf_op | source)
XLA Modules:
  0.0 55.1 jit_solution(4252690043843649533)
XLA Ops:
  0.0 46.4 %gather.1 = (bf16[2,8,8,64,128]{4,3,2,1,0:T(8,128)(2,1)S(1)}, f32[512,3072]{1,0:T(8,128)S(1)}, bf16[3072,2048]{1,0:T(8,128)(2,1)S(1)}) custom-call(bf16[256,8192]{1,0:T(8,128)(2,1)} %act.1, bf16[256,8192]{1,0:T(8,128)(2,1)} %grad.1, bf16[64,8192]{1,0:T(8,128)(2,1)} %bitcast.2, bf16[32,8192]{1,0:T(8,128)(2,1)} %bitcast.3, s32[16]{0:T(128)} %lengths_hbm.1, ...), custom_call_target="tpu_custom_call" | custom-call | tf_op jit(solution)/shard_map/gather/pallas_call | solution.py:235
  46.4 8.7 %score.1 = bf16[1024,3072]{1,0:T(8,128)(2,1)} custom-call(bf16[2,8,8,64,128]{4,3,2,1,0:T(8,128)(2,1)S(1)} %get-tuple-element.8.qa, f32[512,3072]{1,0:T(8,128)S(1)} %get-tuple-element.9.total, bf16[3072,2048]{1,0:T(8,128)(2,1)S(1)} %get-tuple-element.10.store), custom_call_target="tpu_custom_call" | custom-call | tf_op jit(solution)/shard_map/score/pallas_call | solution.py:251

commit v3 on v2

v3 whole, which is shorter than its diff:
```python
import jax
import jax.numpy as jnp
from jax import lax
from jax.experimental import pallas as pl
from jax.experimental.pallas import tpu as pltpu
from jax.sharding import PartitionSpec as P

D = 8192
RIN = 64
ROUT = 32
K = 2048
SEQ = 16
TOK = 256
NSEQ = 16
NP = 8
COLS = 128
HALF = 64
CHUNK = 1024
NCHUNK = D // CHUNK
STORE = 3072
WIDE = 1024
BF = jnp.bfloat16
F32 = jnp.float32
MESH = pl.DeviceIdType.MESH
ACROSS = (((1,), (1,)), ((), ()))


def mod(a, b):
    return lax.rem(a, b)


RING = (0, 1, 3, 2)


def offset(j):
    return RING[j // 2], j % 2


def gather_kernel(act, grad, w_in, w_out, lengths_hbm, factor, store, qb, done, early, store_v,
                  qa, total, fown, act_v, grad_v, w_in_v, w_out_v, fcol, pg, lengths,
                  load_sem, store_sem, length_sem, stage_sem, own_f_sem, f_send, f_recv, p_send, p_recv, s_send, s_recv,
                  af_send, af_recv, bn_send, bn_recv, an_send, an_recv, bf_send, bf_recv,
                  ac_send, ac_recv, bc_send, bc_recv):
    outer = lax.axis_index("outer")
    inner = lax.axis_index("inner")
    core = mod(inner, 2)
    spot = lax.div(inner, 2)
    y, xlo = lax.div(outer, 2), mod(outer, 2)
    z, xhi = lax.div(spot, 2), mod(spot, 2)
    gx = mod(xlo + xhi, 2)
    sibling = (outer, spot * 2 + 1 - core)
    member = y * 2 + gx

    def near(j, flip=0):
        dz, dx = offset(j)
        hi = mod(xhi + dx, 2)
        return y * 2 + mod(gx + hi, 2), (mod(z + dz, 4) * 2 + hi) * 2 + mod(core + flip, 2)

    def far(j):
        dy, dx = offset(j)
        return mod(y + dy, 4) * 2 + mod(gx + dx + xhi, 2), inner

    length_copy = pltpu.make_async_copy(lengths_hbm, lengths, length_sem)
    length_copy.start()
    stages = []
    for n in range(2):
        cols = pl.ds(pl.multiple_of((member * 2 + n) * COLS, COLS), COLS)
        copy = pltpu.make_async_copy(factor.at[:, cols], fown.at[n], stage_sem.at[n])
        copy.start()
        stages.append(copy)
    loads = []
    for k in range(NCHUNK):
        cols = pl.ds(k * CHUNK, CHUNK)
        row = []
        for n, (src, dst) in enumerate(((w_in, w_in_v), (act, act_v), (w_out, w_out_v), (grad, grad_v))):
            copy = pltpu.make_async_copy(src.at[:, cols], dst.at[:, cols], load_sem.at[k, n])
            copy.start()
            row.append(copy)
        loads.append(row)

    barrier = pltpu.get_barrier_semaphore()
    peers = [near(j, flip) for j in range(8) for flip in range(2) if j + flip] + [far(j) for j in range(1, 8)]
    for peer in peers:
        pl.semaphore_signal(barrier, inc=1, device_id=peer, device_id_type=MESH)
    def remote(src, send, recv, target, dst=None):
        return pltpu.make_async_remote_copy(src_ref=src, dst_ref=src if dst is None else dst, send_sem=send, recv_sem=recv,
                                            device_id=target, device_id_type=MESH)

    sends = []

    def go(*args):
        copy = remote(*args)
        copy.start()
        sends.append(copy)
        return copy

    f_copies = []
    ins = jnp.zeros((RIN, TOK), F32)
    outs = jnp.zeros((ROUT, TOK), F32)
    for k in range(NCHUNK):
        cols = pl.ds(k * CHUNK, CHUNK)
        for copy in loads[k]:
            copy.wait()
        if k == 2:
            for copy in stages:
                copy.wait()
            pl.semaphore_wait(barrier, len(peers))
            for n in range(1, 16):
                to = near(n // 2, n % 2)
                f_copies.append(go(fown.at[mod(to[1], 2)], f_send.at[n], f_recv.at[n], to, fcol.at[inner]))
            own_f = pltpu.make_async_copy(fown.at[core], fcol.at[inner], own_f_sem)
            own_f.start()
        if k == NCHUNK - 1:
            store_copy = pltpu.make_async_copy(store, store_v, store_sem)
            store_copy.start()
        ins += lax.dot_general(w_in_v[:, cols], act_v[:, cols], ACROSS, preferred_element_type=F32)
        outs += lax.dot_general(w_out_v[:, cols], grad_v[:, cols], ACROSS, preferred_element_type=F32)
    ins, outs = ins.T, outs.T

    length_copy.wait()
    position = lax.broadcasted_iota(jnp.int32, (SEQ, ROUT), 0)
    kept = [jnp.where(position < lengths[s], outs[s * SEQ:(s + 1) * SEQ], 0.0) for s in range(NSEQ)]
    outs = jnp.concatenate(kept, axis=0).astype(BF)
    ins = jnp.concatenate([ins, ins], axis=1).astype(BF).astype(F32)
    own_slot = xlo * 8 + y * 2 + core
    for j in range(K // 128):
        a = lax.broadcasted_iota(jnp.int32, (ROUT, 128), 0)
        b = lax.broadcasted_iota(jnp.int32, (ROUT, 128), 1)
        pick = jnp.where(a == 2 * j + lax.div(b, RIN), 1.0, 0.0).astype(BF)
        wide = jnp.dot(outs, pick, preferred_element_type=F32)
        sums = jnp.sum((wide * ins).reshape(NP, 2 * SEQ, 128), axis=1)
        pg[own_slot, :, j * 128:(j + 1) * 128] = sums.astype(BF)

    p_copies = [go(pg.at[own_slot], p_send.at[j], p_recv.at[j], far(j)) for j in range(1, 8)]
    s_copies = [go(pg.at[own_slot], s_send.at[0], s_recv.at[0], sibling)]
    for j in range(1, 8):
        p_copies[j - 1].wait_recv()
        dy, dx = offset(j)
        slot = mod(xlo + dx, 2) * 8 + mod(y + 4 - dy, 4) * 2 + core
        s_copies.append(go(pg.at[slot], s_send.at[j], s_recv.at[j], sibling))
    own_f.wait()
    for copy in f_copies:
        copy.wait_recv()
    for copy in s_copies:
        copy.wait_recv()

    white = jnp.dot(pg[...].reshape(16 * NP, K), fcol[...].reshape(K, COLS), preferred_element_type=F32).astype(BF)
    qa[core, spot, member] = white[:HALF]
    qb[core, member, spot] = white[HALF:]

    a_far, b_near = [], []
    for j in range(1, 8):
        a_far.append(go(qa.at[core, spot, member], af_send.at[j], af_recv.at[j], far(j)))
        b_near.append(go(qb.at[core, member, spot], bn_send.at[j], bn_recv.at[j], near(j)))

    def ring(a, h):
        return mod(a + 4 - RING[h], 4)

    def a_batch(h):
        part = qa.at[core, spot, pl.ds(2 * ring(y, h), 2)]
        return [remote(part, an_send.at[h, j], an_recv.at[h, j], near(j)) for j in range(1, 8)]

    def b_batch(h):
        part = qb.at[core, member, pl.ds(2 * ring(z, h), 2)]
        return [remote(part, bf_send.at[h, j], bf_recv.at[h, j], far(j)) for j in range(1, 8)]

    def a_over(h):
        return remote(qa.at[core, :, pl.ds(2 * ring(y, h), 2)], ac_send.at[h], ac_recv.at[h], sibling)

    def b_over(h):
        return remote(qb.at[core, :, pl.ds(2 * ring(z, h), 2)], bc_send.at[h], bc_recv.at[h], sibling)

    a_batches, b_batches, overs = [], [], {}

    def send(h):
        for stage, batches, batch in ((a_far, a_batches, a_batch), (b_near, b_batches, b_batch)):
            for j in (2 * h, 2 * h + 1):
                if j:
                    stage[j - 1].wait_recv()
            batches.append(batch(h))
            for copy in batches[h]:
                copy.start()

    def hand(h):
        for name, batches, over in (("a", a_batches, a_over), ("b", b_batches, b_over)):
            for copy in batches[h]:
                copy.wait_recv()
            overs[name, h] = over(h)
            overs[name, h].start()

    def add(h):
        overs["a", h].wait_recv()
        at = ring(y, h)
        lhs = jnp.concatenate([qa[c, :, 2 * at + hi].reshape(8 * HALF, COLS) for hi in range(2) for c in range(2)], axis=1)
        cols = pl.ds(pl.multiple_of(at * 4 * COLS, 4 * COLS), 4 * COLS)
        for n in range(STORE // WIDE):
            some = slice(n * WIDE, (n + 1) * WIDE)
            part = lax.dot_general(lhs, store_v[some, cols], ACROSS, preferred_element_type=F32)
            if h == 0:
                total[:, some] = part
            elif h < 3:
                total[:, some] += part
            else:
                done[:, :, :, :, some] = (total[:, some] + part).astype(BF).reshape(4, 2, 4, SEQ, WIDE)

    send(0)
    send(1)
    hand(0)
    send(2)
    send(3)
    store_copy.wait()
    add(0)
    hand(1)
    add(1)
    hand(2)
    overs["b", 0].wait_recv()
    overs["b", 1].wait_recv()
    lhs = full_rows(qb, (ring(z, 0), ring(z, 1)))
    for n in range(STORE // WIDE):
        some = slice(n * WIDE, (n + 1) * WIDE)
        part = lax.dot_general(lhs, store_v[some, :], ACROSS, preferred_element_type=F32)
        early[:, :, :, some] = part.astype(BF).reshape(4, 4, SEQ, WIDE)
    hand(3)
    add(2)
    add(3)
    overs["b", 2].wait_recv()
    overs["b", 3].wait_recv()

    for copy in sends + [c for batch in a_batches + b_batches for c in batch] + list(overs.values()):
        copy.wait_send()


def full_rows(qb, ys):
    rows = [jnp.concatenate([qb[c, k, 2 * at + e] for k in range(8) for c in range(2)], axis=1) for at in ys for e in range(2)]
    return jnp.concatenate(rows, axis=0)


def score_kernel(qb, done, early, store, out, late, done_sem, early_sem, late_sem):
    z = lax.div(lax.axis_index("inner"), 4)
    zs = [mod(z + 4 - d, 4) for d in RING]
    copies = []
    for h in range(2):
        for hi in range(2):
            copies.append(pltpu.make_async_copy(early.at[2 * h + hi], out.at[:, 1, zs[h], hi], early_sem.at[h, hi]))
    for y in range(4):
        copies.append(pltpu.make_async_copy(done.at[:, :, y], out.at[y, 0], done_sem.at[y]))
    for copy in copies:
        copy.start()
    lhs = full_rows(qb, zs[2:])
    for n in range(STORE // WIDE):
        some = slice(n * WIDE, (n + 1) * WIDE)
        part = lax.dot_general(lhs, store[some, :], ACROSS, preferred_element_type=F32)
        late[:, :, :, some] = part.astype(BF).reshape(4, 4, SEQ, WIDE)
        for h in range(2):
            for hi in range(2):
                copy = pltpu.make_async_copy(late.at[2 * h + hi, :, :, some], out.at[:, 1, zs[2 + h], hi, :, some], late_sem.at[n, 2 * h + hi])
                copy.start()
                copies.append(copy)
    for copy in copies:
        copy.wait()


def shards(activations, out_grads, proj_in, proj_out, lengths, factor, store):
    dma = pltpu.SemaphoreType.DMA
    hbm = pl.BlockSpec(memory_space=pltpu.HBM)
    vmem = pl.BlockSpec(memory_space=pltpu.VMEM)
    parts = pl.pallas_call(
        gather_kernel,
        out_shape=[pltpu.VMEM((2, 8, 8, HALF, COLS), BF), pltpu.VMEM((4, 2, 4, SEQ, STORE), BF),
                   pltpu.VMEM((4, 4, SEQ, STORE), BF), pltpu.VMEM((STORE, K), BF)],
        in_specs=[hbm] * 7,
        out_specs=[vmem] * 4,
        scratch_shapes=[
            pltpu.VMEM((2, 8, 8, HALF, COLS), BF), pltpu.VMEM((8 * HALF, STORE), F32), pltpu.VMEM((2, 128, COLS), BF),
            pltpu.VMEM((TOK, D), BF), pltpu.VMEM((TOK, D), BF),
            pltpu.VMEM((RIN, D), BF), pltpu.VMEM((ROUT, D), BF),
            pltpu.VMEM((16, 128, COLS), BF), pltpu.VMEM((16, NP, K), BF), pltpu.SMEM((NSEQ,), jnp.int32),
            dma((NCHUNK, 4)), dma, dma, dma((2,)), dma, dma((16,)), dma((16,)),
        ] + [dma((8,))] * 8 + [dma((4, 8))] * 4 + [dma((4,))] * 4,
        compiler_params=pltpu.CompilerParams(collective_id=0, has_side_effects=True, vmem_limit_bytes=36 << 20),
        name="gather",
    )(*[pltpu.with_memory_space_constraint(v, pltpu.HBM)
        for v in (activations, out_grads, proj_in.T, proj_out.T, lengths, factor, store)])
    scores = pl.pallas_call(
        score_kernel,
        out_shape=jax.ShapeDtypeStruct((4, 2, 4, 2, SEQ, STORE), BF),
        in_specs=[vmem] * 4,
        out_specs=hbm,
        scratch_shapes=[pltpu.VMEM((4, 4, SEQ, STORE), BF), dma((4,)), dma((2, 2)), dma((STORE // WIDE, 4))],
        compiler_params=pltpu.CompilerParams(vmem_limit_bytes=24 << 20),
        name="score",
    )(*parts)
    return scores.reshape(16 * HALF, STORE)


def solution(mesh):
    in_specs = (
        P(("outer", "inner"), None),
        P(("outer", "inner"), None),
        P(),
        P(),
        P(("outer", "inner")),
        P("inner", None),
        P(("outer", "inner"), None),
    )
    out_specs = P(None, ("outer", "inner"))
    return jax.shard_map(shards, mesh=mesh, in_specs=in_specs, out_specs=out_specs, check_vma=False)
```

time: 55.2 us -> 49.7 us (0.900)
  Pallas kernels: 55.1 us -> 49.4 us
    pallas_call x1, Pallas kernels: 8.74 us -> 5.03 us  [shards(): pl.pallas_call(score_kernel, out_shape=jax.ShapeDtypeStruct((4, 2, 4, 2,...]
    pallas_call x1, Pallas kernels: 46.4 us -> 44.4 us  [shards(): pl.pallas_call(gather_kernel, out_shape=[pltpu.VMEM((2, 8, 8, HALF, COLS)...]
where the time goes in v3:
time: 49.7 us; the launch traced here: 49.6 us
  Pallas kernels  49.4 us (99%)
    pallas_call x1, Pallas kernels, shards(): pl.pallas_call(gather_kernel, out_shape=[pltpu.VMEM((2, 8, 8, HALF, COLS)...  44.4 us
    pallas_call x1, Pallas kernels, shards(): pl.pallas_call(score_kernel, out_shape=jax.ShapeDtypeStruct((4, 2, 4, 2,...  5.03 us

profile of v3, /device:TPU:1, one launch (start us, length us, event | category | flops | bytes accessed | tf_op | source)
XLA Modules:
  0.0 49.6 jit_solution(9945019561311836956)
XLA Ops:
  0.0 44.4 %gather.1 = (bf16[2,8,8,64,128]{4,3,2,1,0:T(8,128)(2,1)S(1)}, bf16[4,2,4,16,3072]{4,3,2,1,0:T(8,128)(2,1)S(1)}, bf16[4,4,16,3072]{3,2,1,0:T(8,128)(2,1)S(1)}, bf16[3072,2048]{1,0:T(8,128)(2,1)S(1)}) custom-call(bf16[256,8192]{1,0:T(8,128)(2,1)} %act.1, bf16[256,8192]{1,0:T(8,128)(2,1)} %grad.1, bf16[64,8192]{1,0:T(8,128)(2,1)} %bitcast.3, ...), custom_call_target="tpu_custom_call" | custom-call | tf_op jit(solution)/shard_map/gather/pallas_call | solution.py:267
  44.4 5.0 %score.1 = bf16[4,2,4,2,16,3072]{5,4,3,2,1,0:T(8,128)(2,1)} custom-call(bf16[2,8,8,64,128]{4,3,2,1,0:T(8,128)(2,1)S(1)} %get-tuple-element.9.qb, bf16[4,2,4,16,3072]{4,3,2,1,0:T(8,128)(2,1)S(1)} %get-tuple-element.10.done, bf16[4,4,16,3072]{3,2,1,0:T(8,128)(2,1)S(1)} %get-tuple-element.11.early, bf16[3072,2048]{1,0:T(8,128)(2,1)S(1)} %get-tuple-element.12.store), custom_call_target="tpu_custom_call" | custom-call | tf_op jit(solution)/shard_map/score/pallas_call | solution.py:284

commit v4 on v3

--- a/solution.py
+++ b/solution.py
@@ -131,7 +131,7 @@
         sums = jnp.sum((wide * ins).reshape(NP, 2 * SEQ, 128), axis=1)
         pg[own_slot, :, j * 128:(j + 1) * 128] = sums.astype(BF)
 
-    p_copies = [go(pg.at[own_slot], p_send.at[j], p_recv.at[j], far(j)) for j in range(1, 8)]
+    p_copies = [go(pg.at[own_slot], p_send.at[j], p_recv.at[j], far(j)) for j in range(7, 0, -1)][::-1]
     s_copies = [go(pg.at[own_slot], s_send.at[0], s_recv.at[0], sibling)]
     for j in range(1, 8):
         p_copies[j - 1].wait_recv()
@@ -149,9 +149,12 @@
     qb[core, member, spot] = white[HALF:]
 
     a_far, b_near = [], []
-    for j in range(1, 8):
+    for j in range(7, 0, -1):
         a_far.append(go(qa.at[core, spot, member], af_send.at[j], af_recv.at[j], far(j)))
         b_near.append(go(qb.at[core, member, spot], bn_send.at[j], bn_recv.at[j], near(j)))
+
+    a_far.reverse()
+    b_near.reverse()
 
     def ring(a, h):
         return mod(a + 4 - RING[h], 4)

time: 49.7 us -> 50.2 us (1.010)
  no operation moved by 1% of the time
where the time goes in v4:
time: 50.2 us; the launch traced here: 50.1 us
  Pallas kernels  49.9 us (99%)
    pallas_call x1, Pallas kernels, shards(): pl.pallas_call(gather_kernel, out_shape=[pltpu.VMEM((2, 8, 8, HALF, COLS)...  44.9 us
    pallas_call x1, Pallas kernels, shards(): pl.pallas_call(score_kernel, out_shape=jax.ShapeDtypeStruct((4, 2, 4, 2,...  5.03 us

profile of v4, /device:TPU:1, one launch (start us, length us, event | category | flops | bytes accessed | tf_op | source)
XLA Modules:
  0.0 50.1 jit_solution(9580541150519515369)
XLA Ops:
  0.0 44.9 %gather.1 = (bf16[2,8,8,64,128]{4,3,2,1,0:T(8,128)(2,1)S(1)}, bf16[4,2,4,16,3072]{4,3,2,1,0:T(8,128)(2,1)S(1)}, bf16[4,4,16,3072]{3,2,1,0:T(8,128)(2,1)S(1)}, bf16[3072,2048]{1,0:T(8,128)(2,1)S(1)}) custom-call(bf16[256,8192]{1,0:T(8,128)(2,1)} %act.1, bf16[256,8192]{1,0:T(8,128)(2,1)} %grad.1, bf16[64,8192]{1,0:T(8,128)(2,1)} %bitcast.3, ...), custom_call_target="tpu_custom_call" | custom-call | tf_op jit(solution)/shard_map/gather/pallas_call | solution.py:270
  44.9 5.0 %score.1 = bf16[4,2,4,2,16,3072]{5,4,3,2,1,0:T(8,128)(2,1)} custom-call(bf16[2,8,8,64,128]{4,3,2,1,0:T(8,128)(2,1)S(1)} %get-tuple-element.9.qb, bf16[4,2,4,16,3072]{4,3,2,1,0:T(8,128)(2,1)S(1)} %get-tuple-element.10.done, bf16[4,4,16,3072]{3,2,1,0:T(8,128)(2,1)S(1)} %get-tuple-element.11.early, bf16[3072,2048]{1,0:T(8,128)(2,1)S(1)} %get-tuple-element.12.store), custom_call_target="tpu_custom_call" | custom-call | tf_op jit(solution)/shard_map/score/pallas_call | solution.py:287
